TPU v7x, 32 devices: a whole 2x2x4 slice. The times are simulated.
32 devices in a mesh: rep: 2 (over y), grp: 8 (over z, x), tp: 2 (over core).
Axes of the slice: x: 2, y: 2, z: 4, core: 2. Of those that a mesh axis runs over, the one named last changes fastest.
Arguments:
- counts: int32 [16], P(('rep', 'grp')), parts along dimension 0, may hold values from 1 to 8, as said below
- hop_offsets: int32 [128], P(('rep', 'grp')), parts along dimension 0, may hold values from -2 to 2, as said below
- write_pos: int32 [128], P(('rep', 'grp')), parts along dimension 0, may hold values from 0 to 123
- kv_cache: bfloat16 [128, 2, 128, 1024], P(('rep', 'grp'), None, None, 'tp'), parts along dimension 0, may hold values from -27 to 27
- queries: bfloat16 [128, 2, 8192], P(('rep', 'grp'), None, 'tp'), parts along dimension 0, may hold values from -6 to 6
- fresh_kv: bfloat16 [128, 2, 2, 1024], P(('rep', 'grp'), None, None, 'tp'), parts along dimension 0, may hold values from -6 to 6
Outputs:
- new_cache: bfloat16 [128, 2, 128, 1024], P(('rep', 'grp'), None, None, 'tp'), parts along dimension 0
- attended: bfloat16 [128, 2, 8192], P(('rep', 'grp'), None, 'tp'), parts along dimension 0
- served: int32 [16], P('rep'), parts along dimension 0
There are 2 independent parts, one for each index of `rep`. A program takes and returns all parts, laid end to end along the dimension named above; each array names one. Nothing has to cross between parts.
Inputs may be any that keep to these rules, and one draw needn't show every extreme that they name: `counts`: live streams fill a group's first slots; some group holds 8 streams; groups that send hold 8 streams, the others 1 or 2. `hop_offsets`: zero for empty slots and staying streams. A group sends at most one stream with each offset, and no group holds more than 8 streams after the move; offsets -2 and 2 occur.
All inputs are finite; a program needn't handle non-finite values.
Results may differ from a plain program's by a relative error of at most 0.0049.
Values may be sent and summed in bfloat16 or wider, within the bound.
No kernel may reach another device: no remote copies, remote signals or barrier semaphores. Data moves between devices by JAX's collectives and lax.ppermute only.
A program may use at most 64 MiB of HBM per device.

v0:
```python
import jax
import jax.numpy as jnp
from jax import lax
from jax.sharding import PartitionSpec as P

HEAD_DIM = 128
SINK = 4
REACH = 2


def for_sending(x):

    def short(part):
        return part.astype(jnp.bfloat16) if part.dtype == jnp.float32 else part

    return jax.tree.map(short, x)


def shifted(block, axis, distance):
    devices = range(lax.axis_size(axis))
    route = [((i - distance) % len(devices), i) for i in devices]
    return lax.ppermute(block, axis, route)


def decode_rows(cache_rows, positions, query_rows, fresh_rows):
    row_count, _, cache_len, kv_width = cache_rows.shape
    group_count = kv_width // HEAD_DIM
    head_count = query_rows.shape[-1] // HEAD_DIM
    group_size = head_count // group_count
    window = cache_len - SINK
    columns = jnp.arange(cache_len, dtype=jnp.int32)
    outputs = []
    current = cache_rows
    for step_index in range(2):
        target = (SINK + (positions + step_index) % window).astype(jnp.int32)
        row_hit = (columns[None, :] == target[:, None])[:, None, :, None]
        current = jnp.where(row_hit, fresh_rows[:, :, step_index][:, :, None, :], current)
        key_rows = current[:, 0].reshape(row_count, cache_len, group_count, HEAD_DIM)
        values = current[:, 1].reshape(row_count, cache_len, group_count, HEAD_DIM)
        query_now = query_rows[:, step_index].reshape(row_count, group_count, group_size, HEAD_DIM)
        scores = jnp.einsum(
            "rgkd,rlgd->rgkl", query_now, key_rows, preferred_element_type=jnp.float32
        ) * HEAD_DIM ** (-0.5)
        weights = jax.nn.softmax(scores, axis=-1).astype(jnp.bfloat16)
        mixed_heads = jnp.einsum(
            "rgkl,rlgd->rgkd", weights, values, preferred_element_type=jnp.float32
        )
        outputs.append(mixed_heads.astype(jnp.bfloat16).reshape(row_count, head_count * HEAD_DIM))
    return (current, jnp.stack(outputs, axis=1))


def per_device(counts, hop_offsets, write_pos, kv_cache, queries, fresh_kv):
    slot_count = kv_cache.shape[0]
    slot_index = jnp.arange(slot_count, dtype=jnp.int32)
    is_live = slot_index < counts[0]
    moving = jnp.where(is_live, hop_offsets, 0)
    staying = is_live & (moving == 0)
    stay_rank = jnp.cumsum(staying.astype(jnp.int32)) - 1
    running = jnp.sum(staying.astype(jnp.int32))
    offsets = [offset for offset in range(-REACH, REACH + 1) if offset != 0]
    arrived = {}
    for direction in (-1, 1):
        row_pieces = []
        pos_pieces = []
        for distance in range(1, REACH + 1):
            chosen = moving == direction * distance
            outgoing_present = jnp.any(chosen)
            picked = jnp.sum(jnp.where(chosen, slot_index, 0))
            rows_out = lax.dynamic_slice_in_dim(kv_cache, picked, 1, 0)
            pos_out = jnp.where(
                outgoing_present, lax.dynamic_slice_in_dim(write_pos, picked, 1, 0), -1
            )
            row_pieces.append(rows_out)
            pos_pieces.append(pos_out)
        carried = (jnp.concatenate(row_pieces, axis=0), jnp.concatenate(pos_pieces, axis=0))
        for distance in range(1, REACH + 1):
            carried = shifted((carried[0], for_sending(carried[1])), "grp", direction)
            arrived[direction * distance] = (carried[0][:1], carried[1][:1])
            carried = (carried[0][1:], carried[1][1:])
    arrived_rows = jnp.concatenate([arrived[offset][0] for offset in offsets], axis=0)
    arrived_pos = jnp.concatenate([arrived[offset][1] for offset in offsets], axis=0)
    present = arrived_pos >= 0
    arrive_rank = running + jnp.cumsum(present.astype(jnp.int32)) - 1
    served_here = running + jnp.sum(present.astype(jnp.int32))
    pool_dest = jnp.concatenate(
        [jnp.where(staying, stay_rank, -1), jnp.where(present, arrive_rank, -1)]
    )
    pool_index = jnp.arange(pool_dest.shape[0], dtype=jnp.int32)
    matches = pool_dest[None, :] == slot_index[:, None]
    filled = jnp.any(matches, axis=1)
    source = jnp.sum(jnp.where(matches, pool_index[None, :], 0), axis=1)
    pool_rows = jnp.concatenate([kv_cache, arrived_rows], axis=0)
    pool_pos = jnp.concatenate([write_pos, arrived_pos], axis=0)
    placed = jnp.take(pool_rows, source, axis=0)
    placed_pos = jnp.take(pool_pos, source)
    result_cache, result_heads = decode_rows(placed, placed_pos, queries, fresh_kv)
    new_cache = jnp.where(filled[:, None, None, None], result_cache, jnp.zeros((), jnp.bfloat16))
    attended = jnp.where(filled[:, None, None], result_heads, jnp.zeros((), jnp.bfloat16))
    served = lax.all_gather(served_here.reshape(1), "grp", axis=0, tiled=True)
    return (new_cache, attended, served)


def solution(mesh):
    return jax.shard_map(
        per_device,
        mesh=mesh,
        in_specs=(
            P(("rep", "grp")),
            P(("rep", "grp")),
            P(("rep", "grp")),
            P(("rep", "grp"), None, None, "tp"),
            P(("rep", "grp"), None, "tp"),
            P(("rep", "grp"), None, None, "tp"),
        ),
        out_specs=(P(("rep", "grp"), None, None, "tp"), P(("rep", "grp"), None, "tp"), P("rep")),
        check_vma=False,
    )
```

profile of v0, /device:TPU:0, one launch (start us, length us, event | category | flops | bytes accessed | tf_op | source)
XLA Modules:
  0.0 102.7 jit_solution(8830002538838391713)
XLA Ops:
  10.6 1.4 %constant_dynamic-slice_fusion.1 = (bf16[1,2,128,512]{3,2,1,0:T(8,128)(2,1)S(1)}, bf16[1,2,128,512]{3,2,1,0:T(8,128)(2,1)S(1)}, bf16[1,2,128,512]{3,2,1,0:T(8,128)(2,1)S(1)}, bf16[1,2,128,512]{3,2,1,0:T(8,128)(2,1)S(1)}) fusion(bf16[8,2,128,512]{3,2,1,0:T(8,128)(2,1)} %param.9, s32[]{:T(128)S(6)} %select_n.154, s32[]{:T(128)S(6)} %select_n.150, ...), kind=kLoop, calls=%fused_computation.62 | loop fusion | bytes 2097168 | tf_op jit(solution)/shard_map/dynamic_slice | solution.py:69
  12.9 6.0 %collective-permute-start.4 = (bf16[2,2,128,512]{3,2,1,0:T(8,128)(2,1)}, bf16[2,2,128,512]{3,2,1,0:T(8,128)(2,1)}, u32[]{:S(2)}, u32[]{:S(2)}) collective-permute-start(bf16[2,2,128,512]{3,2,1,0:T(8,128)(2,1)} %pad_maximum_fusion), channel_id=1, source_target_pairs={{2,0},{4,2},{6,4},{8,6},{10,8},{12,10},{14,12},{0,14},{3,1},{5,3},... | collective-permute-start | bytes 1572872 | tf_op jit(solution)/shard_map/ppermute | solution.py:22
  23.8 4.7 %collective-permute-start = (s32[2]{0:T(128)S(1)}, s32[2]{0:T(128)S(1)}, u32[]{:S(2)}, u32[]{:S(2)}) collective-permute-start(s32[2]{0:T(128)S(1)} %pad_add_fusion), channel_id=1, source_target_pairs={{2,0},{4,2},{6,4},{8,6},{10,8},{12,10},{14,12},{0,14},{3,1},{5,3},... | collective-permute-start | bytes 32 | tf_op jit(solution)/shard_map/ppermute | solution.py:22
  34.4 5.0 %collective-permute-done = s32[2]{0:T(128)S(1)} collective-permute-done((s32[2]{0:T(128)S(1)}, s32[2]{0:T(128)S(1)}, u32[]{:S(2)}, u32[]{:S(2)}) %collective-permute-start) | collective-permute-done | bytes 40 | tf_op jit(solution)/shard_map/ppermute | solution.py:22
  40.0 2.8 %collective-permute-start.1 = (s32[1]{0:T(128)}, s32[1]{0:T(128)}, u32[]{:S(2)}, u32[]{:S(2)}) collective-permute-start(s32[1]{0:T(128)} %get-tuple-element.37), channel_id=1, source_target_pairs={{2,0},{4,2},{6,4},{8,6},{10,8},{12,10},{14,12},{0,14},{3,1},{5,3},... | collective-permute-start | bytes 20 | tf_op jit(solution)/shard_map/ppermute | solution.py:22
  44.2 5.6 %collective-permute-done.3 = s32[1]{0:T(128)} collective-permute-done((s32[1]{0:T(128)}, s32[1]{0:T(128)}, u32[]{:S(2)}, u32[]{:S(2)}) %collective-permute-start.3) | collective-permute-done | bytes 36 | tf_op jit(solution)/shard_map/ppermute | solution.py:22
  49.8 2.6 %compare_convert_fusion = s32[4,1]{0,1:T(1,128)S(1)} fusion(s32[1,1]{0,1:T(1,128)} %bitcast.10, s32[1,1]{0,1:T(1,128)} %bitcast.9, s32[1,1]{0,1:T(1,128)} %bitcast.8, s32[1,1]{0,1:T(1,128)} %bitcast.7), kind=kLoop, calls=%fused_computation.48 | loop fusion | flops 20 | bytes 32 | tf_op jit(solution)/shard_map/convert_element_type | solution.py:83
  52.7 3.3 %fusion.19 = (s32[]{:T(128)}, s32[4]{0:T(128)S(1)}) fusion(s32[1]{0:T(128)} %collective-permute-done.3, s32[1]{0:T(128)} %get-tuple-element.43, s32[1]{0:T(128)} %get-tuple-element.38, s32[1]{0:T(128)} %collective-permute-done.1), kind=kLoop, calls=%fused_computation.69 | loop fusion | flops 23 | bytes 36 | tf_op jit(solution)/shard_map/reduce_sum | solution.py:84
  56.7 2.7 %concatenate.51 = s32[12]{0:T(128)S(1)} concatenate(s32[8]{0:T(128)S(1)} %copy-done.4, s32[1]{0:T(128)} %collective-permute-done.1, s32[1]{0:T(128)} %get-tuple-element.38, s32[1]{0:T(128)} %get-tuple-element.43, s32[1]{0:T(128)} %collective-permute-done.3), dimensions={0} | concatenate | bytes 96 | tf_op jit(solution)/shard_map/concatenate | solution.py:93
  60.7 1.7 %slice.68 = bf16[1,2,128,512]{3,2,1,0:T(8,128)(2,1)} slice(bf16[2,2,128,512]{3,2,1,0:T(8,128)(2,1)} %collective-permute-done.4), slice={[1:2], [0:2], [0:128], [0:512]} | slice | bytes 524288 | tf_op jit(solution)/shard_map/slice | solution.py:79
  62.4 1.2 %fusion.21 = s32[8]{0:T(128)} fusion(pred[8]{0:T(512)(128)(4,1)S(1)} %get-tuple-element.19, s32[8]{0:T(128)} %copy-done.9), kind=kLoop, calls=%fused_computation.71 | loop fusion | flops 64 | bytes 72 | tf_op jit(solution)/shard_map/add | solution.py:35
  65.2 1.8 %dynamic-update-slice = s32[8]{0:T(128)} dynamic-update-slice(s32[8]{0:T(128)} %broadcast_in_dim.111, s32[1]{0:T(128)} %bitcast.22, u32[]{:T(128)} %bitcast.23) | dynamic-update-slice | bytes 12
  67.0 1.3 %iota_compare_fusion = pred[8,128]{1,0:T(8,128)(4,1)} fusion(s32[8]{0:T(128)} %fusion.21), kind=kLoop, calls=%fused_computation.38 | loop fusion | flops 1024 | bytes 1056 | tf_op jit(solution)/shard_map/eq | solution.py:36
  70.0 1.8 %fusion.25 = (bf16[1,2,128,512]{3,2,1,0:T(8,128)(2,1)}, bf16[12,2,128,512]{3,2,1,0:T(8,128)(2,1)S(1)}) fusion(bf16[2,2,128,512]{3,2,1,0:T(8,128)(2,1)} %collective-permute-done.6, bf16[12,2,128,512]{3,2,1,0:T(8,128)(2,1)S(1)} %slice_dynamic-update-slice_fusion.1), kind=kLoop, calls=%fused_computation.83 | loop fusion | bytes 1048576 | tf_op jit(solution)/shard_map/slice | solution.py:79
  71.7 1.3 %collective-permute-start.7 = (bf16[1,2,128,512]{3,2,1,0:T(8,128)(2,1)}, bf16[1,2,128,512]{3,2,1,0:T(8,128)(2,1)S(1)}, u32[]{:S(2)}, u32[]{:S(2)}) collective-permute-start(bf16[1,2,128,512]{3,2,1,0:T(8,128)(2,1)} %get-tuple-element.31), channel_id=1, source_target_pairs={{14,0},{0,2},{2,4},{4,6},{6,8},{8,10},{10,12},{12,14},{15,1},{1,3}... | collective-permute-start | bytes 786440 | tf_op jit(solution)/shard_map/ppermute | solution.py:22
  73.8 10.6 %all-reduce = s32[8]{0:T(128)} all-reduce(s32[8]{0:T(128)} %dynamic-update-slice), channel_id=1, replica_groups=mesh['rep'=2,'grp'=8,'tp'=2] {'grp'}, use_global_device_ids=true, to_apply=%add | all-reduce | flops 8 | bytes 64
  84.4 1.3 %iota_compare_fusion.1 = pred[8,128]{1,0:T(8,128)(4,1)} fusion(s32[8]{0:T(128)} %get-tuple-element.18), kind=kLoop, calls=%fused_computation.40 | loop fusion | flops 1024 | bytes 1056 | tf_op jit(solution)/shard_map/eq | solution.py:36
  85.7 2.1 %gather_fusion.1 = bf16[8,2,128,512]{3,2,1,0:T(8,128)(2,1)} fusion(bf16[12,2,128,512]{3,2,1,0:T(8,128)(2,1)S(1)} %constant_dynamic-update-slice_fusion, s32[1024]{0:T(1024)} %copy-done.5), kind=kCustom, calls=%fused_computation.1 | custom fusion | bytes 4194336 | tf_op jit(solution)/shard_map/jit(_take)/gather | solution.py:94
  87.9 2.9 %broadcast_select_fusion = (bf16[8,2,128,512]{3,2,1,0:T(8,128)(2,1)}, bf16[8,2,128,512]{3,2,1,0:T(8,128)(2,1)S(1)}, bf16[8,2,128,512]{3,2,1,0:T(8,128)(2,1)S(1)}) fusion(pred[8]{0:T(512)(128)(4,1)S(1)} %copy-done.6, bf16[8,2,512]{2,1,0:T(2,128)(2,1)S(1)} %copy.26, pred[8,128]{1,0:T(8,128)(4,1)S(1)} %copy-done.11, bf16[8,2,128,512]{3,2,1,0:T(8,128)(2,1)} %gather_fusion.1, ...), kind=kLoop, calls=%fused_computation.5 | loop fusion | flops 4194304 | bytes 8423440 | tf_op jit(solution)/shard_map/jit(_where)/select_n | solution.py:97
  90.7 1.6 %fusion.23 = (bf16[8,1,128,512]{3,2,1,0:T(8,128)(2,1)}, bf16[8,1,128,512]{3,2,1,0:T(8,128)(2,1)}) fusion(bf16[8,2,128,512]{3,2,1,0:T(8,128)(2,1)S(1)} %get-tuple-element.17), kind=kLoop, calls=%fused_computation.81 | loop fusion | bytes 4194304 | tf_op jit(solution)/shard_map/slice | solution.py:38
  92.3 1.6 %copy.29 = bf16[8,1,128,512]{2,3,0,1:T(8,128)(2,1)S(1)} copy(bf16[8,1,128,512]{3,2,1,0:T(8,128)(2,1)} %get-tuple-element.23) | data formatting | bytes 2097152 | tf_op jit(solution)/shard_map/slice | solution.py:38
  94.5 1.6 %copy.31 = bf16[8,1,128,512]{2,3,0,1:T(8,128)(2,1)S(1)} copy(bf16[8,1,128,512]{3,2,1,0:T(8,128)(2,1)} %get-tuple-element.24) | data formatting | bytes 2097152 | tf_op jit(solution)/shard_map/slice | solution.py:39
  96.9 1.2 %fusion.24 = (bf16[8,1,128,512]{3,2,1,0:T(8,128)(2,1)}, bf16[8,1,128,512]{3,2,1,0:T(8,128)(2,1)S(1)}) fusion(bf16[8,2,128,512]{3,2,1,0:T(8,128)(2,1)S(1)} %get-tuple-element.16), kind=kLoop, calls=%fused_computation.82 | loop fusion | bytes 4194304 | tf_op jit(solution)/shard_map/slice | solution.py:38
  98.1 1.6 %copy.33 = bf16[8,1,128,512]{2,3,0,1:T(8,128)(2,1)S(1)} copy(bf16[8,1,128,512]{3,2,1,0:T(8,128)(2,1)} %get-tuple-element.25) | data formatting | bytes 2097152 | tf_op jit(solution)/shard_map/slice | solution.py:38
  (82 shorter events, 19.4 us)
Async XLA Ops:
  10.6 9.9 %copy-start.4 = (s32[8]{0:T(128)S(1)}, s32[8]{0:T(128)}, u32[]{:S(2)}) copy-start(s32[8]{0:T(128)} %param.8) | copy-start | bytes 100
  10.6 20.5 %copy-start = (bf16[8,2,128,512]{3,2,1,0:T(8,128)(2,1)S(1)}, bf16[8,2,128,512]{3,2,1,0:T(8,128)(2,1)}, u32[]{:S(2)}) copy-start(bf16[8,2,128,512]{3,2,1,0:T(8,128)(2,1)} %param.9) | copy-start | bytes 6291460
  12.9 47.7 %collective-permute-start.4 = (bf16[2,2,128,512]{3,2,1,0:T(8,128)(2,1)}, bf16[2,2,128,512]{3,2,1,0:T(8,128)(2,1)}, u32[]{:S(2)}, u32[]{:S(2)}) collective-permute-start(bf16[2,2,128,512]{3,2,1,0:T(8,128)(2,1)} %pad_maximum_fusion), channel_id=1, source_target_pairs={{2,0},{4,2},{6,4},{8,6},{10,8},{12,10},{14,12},{0,14},{3,1},{5,3},... | collective-permute-start | bytes 1572872 | tf_op jit(solution)/shard_map/ppermute | solution.py:22
  19.7 50.2 %collective-permute-start.6 = (bf16[2,2,128,512]{3,2,1,0:T(8,128)(2,1)}, bf16[2,2,128,512]{3,2,1,0:T(8,128)(2,1)}, u32[]{:S(2)}, u32[]{:S(2)}) collective-permute-start(bf16[2,2,128,512]{3,2,1,0:T(8,128)(2,1)} %pad_maximum_fusion.1), channel_id=1, source_target_pairs={{14,0},{0,2},{2,4},{4,6},{6,8},{8,10},{10,12},{12,14},{15,1},{1,3}... | collective-permute-start | bytes 1572872 | tf_op jit(solution)/shard_map/ppermute | solution.py:22
  23.8 15.6 %collective-permute-start = (s32[2]{0:T(128)S(1)}, s32[2]{0:T(128)S(1)}, u32[]{:S(2)}, u32[]{:S(2)}) collective-permute-start(s32[2]{0:T(128)S(1)} %pad_add_fusion), channel_id=1, source_target_pairs={{2,0},{4,2},{6,4},{8,6},{10,8},{12,10},{14,12},{0,14},{3,1},{5,3},... | collective-permute-start | bytes 32 | tf_op jit(solution)/shard_map/ppermute | solution.py:22
  31.1 0.8 copy-start.2
  31.1 1.5 %copy-start.1 = (bf16[8,2,4096]{2,1,0:T(2,128)(2,1)S(1)}, bf16[8,2,4096]{2,1,0:T(2,128)(2,1)}, u32[]{:S(2)}) copy-start(bf16[8,2,4096]{2,1,0:T(2,128)(2,1)} %param.10) | copy-start | bytes 393220
  31.1 2.6 %copy-start.12 = (u32[32]{0:T(128)S(1)}, u32[32]{0:T(128)}, u32[]{:S(2)}) copy-start(u32[32]{0:T(128)} %constant.89) | copy-start | bytes 388
  31.1 11.7 %collective-permute-start.2 = (s32[2]{0:T(128)S(1)}, s32[2]{0:T(128)S(1)}, u32[]{:S(2)}, u32[]{:S(2)}) collective-permute-start(s32[2]{0:T(128)S(1)} %pad_add_fusion.1), channel_id=1, source_target_pairs={{14,0},{0,2},{2,4},{4,6},{6,8},{8,10},{10,12},{12,14},{15,1},{1,3}... | collective-permute-start | bytes 32 | tf_op jit(solution)/shard_map/ppermute | solution.py:22
  40.0 4.2 %collective-permute-start.1 = (s32[1]{0:T(128)}, s32[1]{0:T(128)}, u32[]{:S(2)}, u32[]{:S(2)}) collective-permute-start(s32[1]{0:T(128)} %get-tuple-element.37), channel_id=1, source_target_pairs={{2,0},{4,2},{6,4},{8,6},{10,8},{12,10},{14,12},{0,14},{3,1},{5,3},... | collective-permute-start | bytes 20 | tf_op jit(solution)/shard_map/ppermute | solution.py:22
  43.4 6.4 %collective-permute-start.3 = (s32[1]{0:T(128)}, s32[1]{0:T(128)}, u32[]{:S(2)}, u32[]{:S(2)}) collective-permute-start(s32[1]{0:T(128)} %get-tuple-element.44), channel_id=1, source_target_pairs={{14,0},{0,2},{2,4},{4,6},{6,8},{8,10},{10,12},{12,14},{15,1},{1,3}... | collective-permute-start | bytes 20 | tf_op jit(solution)/shard_map/ppermute | solution.py:22
  56.6 4.1 %copy-start.13 = (s32[12]{0:T(128)}, s32[12]{0:T(128)S(1)}, u32[]{:S(2)}) copy-start(s32[12]{0:T(128)S(1)} %pad_add_fusion.3) | copy-start | bytes 148
  59.4 1.3 %copy-start.5 = (s32[1024]{0:T(1024)}, s32[1024]{0:T(1024)S(1)}, u32[]{:S(2)}) copy-start(s32[1024]{0:T(1024)S(1)} %pad_clamp_fusion) | copy-start | bytes 12292
  60.0 0.6 copy-start.9
  60.7 1.7 %copy-start.7 = (pred[8]{0:T(512)(128)(4,1)}, pred[8]{0:T(512)(128)(4,1)S(1)}, u32[]{:S(2)}) copy-start(pred[8]{0:T(512)(128)(4,1)S(1)} %get-tuple-element.19) | copy-start | bytes 28
  62.4 6.6 %collective-permute-start.5 = (bf16[1,2,128,512]{3,2,1,0:T(8,128)(2,1)}, bf16[1,2,128,512]{3,2,1,0:T(8,128)(2,1)S(1)}, u32[]{:S(2)}, u32[]{:S(2)}) collective-permute-start(bf16[1,2,128,512]{3,2,1,0:T(8,128)(2,1)} %slice.68), channel_id=1, source_target_pairs={{2,0},{4,2},{6,4},{8,6},{10,8},{12,10},{14,12},{0,14},{3,1},{5,3},... | collective-permute-start | bytes 786440 | tf_op jit(solution)/shard_map/ppermute | solution.py:22
  67.0 6.1 %copy-start.14 = (s32[12]{0:T(128)S(1)}, s32[12]{0:T(128)}, u32[]{:S(2)}) copy-start(s32[12]{0:T(128)} %copy-done.13) | copy-start | bytes 148
  71.7 13.9 %collective-permute-start.7 = (bf16[1,2,128,512]{3,2,1,0:T(8,128)(2,1)}, bf16[1,2,128,512]{3,2,1,0:T(8,128)(2,1)S(1)}, u32[]{:S(2)}, u32[]{:S(2)}) collective-permute-start(bf16[1,2,128,512]{3,2,1,0:T(8,128)(2,1)} %get-tuple-element.31), channel_id=1, source_target_pairs={{14,0},{0,2},{2,4},{4,6},{6,8},{8,10},{10,12},{12,14},{15,1},{1,3}... | collective-permute-start | bytes 786440 | tf_op jit(solution)/shard_map/ppermute | solution.py:22
  85.7 2.2 %copy-start.3 = (bf16[8,2,512]{2,1,0:T(2,128)(2,1)S(1)}, bf16[8,2,512]{2,1,0:T(2,128)(2,1)}, u32[]{:S(2)}) copy-start(bf16[8,2,512]{2,1,0:T(2,128)(2,1)} %copy.28) | copy-start | bytes 49156
  85.7 2.2 %copy-start.6 = (pred[8]{0:T(512)(128)(4,1)S(1)}, pred[8]{0:T(512)(128)(4,1)}, u32[]{:S(2)}) copy-start(pred[8]{0:T(512)(128)(4,1)} %fusion.14) | copy-start | bytes 28
  85.7 2.2 %copy-start.8 = (pred[8]{0:T(512)(128)(4,1)S(1)}, pred[8]{0:T(512)(128)(4,1)}, u32[]{:S(2)}) copy-start(pred[8]{0:T(512)(128)(4,1)} %copy-done.7) | copy-start | bytes 28
  85.7 2.2 %copy-start.10 = (pred[8,128]{1,0:T(8,128)(4,1)S(1)}, pred[8,128]{1,0:T(8,128)(4,1)}, u32[]{:S(2)}) copy-start(pred[8,128]{1,0:T(8,128)(4,1)} %iota_compare_fusion) | copy-start | bytes 3076
  85.7 2.2 %copy-start.11 = (pred[8,128]{1,0:T(8,128)(4,1)S(1)}, pred[8,128]{1,0:T(8,128)(4,1)}, u32[]{:S(2)}) copy-start(pred[8,128]{1,0:T(8,128)(4,1)} %iota_compare_fusion.1) | copy-start | bytes 3076
where the time goes:
time: 103 us
  local copies, waits for them, and re-layouts  26.3 us (26%)
  other arithmetic  21 us (20%)
  between operations  15.6 us (15%)
  starting transfers between devices  14.9 us (14%)
  waiting for transfers between devices  12.1 us (12%)
  blocking collectives  10.6 us (10%)
  matrix products  2.14 us (2%)
    ppermute x8, starting transfers between devices, shifted(): return lax.ppermute(block, axis, route)  14.9 us
    ppermute x8, waiting for transfers between devices, shifted(): return lax.ppermute(block, axis, route)  12.1 us
    unnamed x1, blocking collectives  10.6 us
    slice x4, local copies, waits for them, and re-layouts, decode_rows(): current[:, 0].reshape(row_count, cache_len, group_count, HEAD_DIM)  5.96 us
    slice x3, local copies, waits for them, and re-layouts, per_device(): carried = (carried[0][1:], carried[1][1:])  4.11 us
    unnamed x35, local copies, waits for them, and re-layouts  3.98 us
    reduce_sum x1, other arithmetic, per_device(): served_here = running + jnp.sum(present.astype(jnp.int32))  3.3 us
    select_n x1, other arithmetic, per_device(): jnp.where(filled[:, None, None, None], result_cache, jnp.zeros((), jnp.bf...  2.85 us
  transfers between devices with their start and end apart: 8, of which 4 were waited for; matrix products, arithmetic and copies ran while one was open for 26% of the time, Pallas kernels for 0%

commit v1 on v0

v1 whole, which is shorter than its diff:
```python
import functools

import jax
import jax.numpy as jnp
from jax import lax
from jax.experimental import pallas as pl
from jax.experimental.pallas import tpu as pltpu
from jax.sharding import PartitionSpec as P

HEAD_DIM = 128
SINK = 4
REACH = 2
STEPS = 2
OFFSETS = tuple(o for o in range(-REACH, REACH + 1) if o != 0)
ORDER = (1, -1, 2, -2)
NEAR = (1, -1)
HEADER = 16
LANES = 128
STAY = 0
SENT = 1
POS = SENT + len(OFFSETS)
VMEM_LIMIT = 32 * 1024 * 1024

VMEM_SPEC = pl.BlockSpec(memory_space=pltpu.VMEM)
SMEM_SPEC = pl.BlockSpec(memory_space=pltpu.SMEM)
ANY_SPEC = pl.BlockSpec(memory_space=pl.ANY)
HBM_SPEC = pl.BlockSpec(memory_space=pltpu.HBM)


def shifted(block, distance):
    count = lax.axis_size("grp")
    return lax.ppermute(block, "grp", [(i, (i + distance) % count) for i in range(count)])


def relay_shifts(groups):
    known = {0, *(-o % groups for o in NEAR)}
    late = {-o % groups for o in OFFSETS}
    shifts = []
    while len(known | late) < groups:
        best = max(range(1, groups), key=lambda d: len(known | {(k - d) % groups for k in known} | late))
        known |= {(k - best) % groups for k in known}
        shifts.append(best)
    return shifts


def load_plan(sources, targets, sem):
    copies = [pltpu.make_async_copy(a, b, sem) for a, b in zip(sources, targets)]
    for copy in copies:
        copy.start()
    for copy in copies:
        copy.wait()


def row_iota(shape):
    return lax.broadcasted_iota(jnp.int32, shape, 0)


def lane_iota(shape):
    return lax.broadcasted_iota(jnp.int32, shape, len(shape) - 1)


def head_lanes(head):
    return slice(head * HEAD_DIM, (head + 1) * HEAD_DIM)


def block_rows(cache_len, head, side):
    return slice((2 * head + side) * cache_len, (2 * head + side + 1) * cache_len)


def pack_kernel(counts, hops_in, positions_in, kv, *refs):
    blocks, own = refs[: len(ORDER)], refs[len(ORDER)]
    hops, positions, plan_sem, sems = refs[len(ORDER) + 1 :]
    load_plan((hops_in, positions_in), (hops, positions), plan_sem)
    slots, _, cache_len, width = kv.shape
    live = counts[0]
    moves = [jnp.where(s < live, hops[s], 0) for s in range(slots)]
    picks, sents = {}, {}

    def pieces(k, pick):
        for head in range(width // HEAD_DIM):
            for side in range(2):
                yield pltpu.make_async_copy(
                    kv.at[pick, side, :, head_lanes(head)],
                    blocks[k].at[block_rows(cache_len, head, side)],
                    sems.at[k],
                )

    for k, offset in enumerate(ORDER):
        pick = jnp.int32(0)
        sent = jnp.int32(0)
        for s in range(slots):
            hit = moves[s] == offset
            pick = jnp.where(hit, s, pick)
            sent = jnp.where(hit, 1, sent)
        picks[offset], sents[offset] = pick, sent
        for piece in pieces(k, pick):
            piece.start()
    stay = jnp.int32(0)
    for s in range(slots):
        stay = stay + jnp.where((s < live) & (moves[s] == 0), 1, 0)
    shape = (HEADER, LANES)
    lane = lane_iota(shape)
    shared = jnp.where(lane == STAY, stay, 0)
    for k, offset in enumerate(OFFSETS):
        shared = jnp.where(lane == SENT + k, sents[offset], shared)
    own[...] = shared
    for k, offset in enumerate(ORDER):
        header = jnp.where(lane == POS, positions[picks[offset]], shared)
        blocks[k][-HEADER:, :] = header.astype(jnp.float32).astype(jnp.bfloat16)
    for k in range(len(ORDER)):
        for piece in pieces(k, 0):
            piece.wait()


def header_of(block):
    return block[-HEADER:, :].astype(jnp.float32).astype(jnp.int32)


def with_row(table, group, header):
    return jnp.where(row_iota(table.shape) == group, header[0:1], table)


def relay_kernel(own, *refs):
    blocks, table = refs[: len(NEAR)], refs[len(NEAR)]
    groups = table.shape[0]
    here = lax.axis_index("grp")
    rows = with_row(jnp.zeros(table.shape, jnp.int32), here, own[...])
    for offset, block in zip(NEAR, blocks):
        rows = with_row(rows, lax.rem(here - offset + groups, groups), header_of(block))
    table[...] = rows


def attend(load, keep, position, queries, fresh, store):
    width = fresh.shape[-1]
    group_size = queries.shape[-1] // width
    cache_len = load(0, 0).shape[0]
    window = cache_len - SINK
    first = SINK + lax.rem(position, window)
    second = SINK + lax.rem(position + 1, window)
    row = row_iota((cache_len, HEAD_DIM))
    score_shape = (group_size * STEPS, cache_len)
    stale = (row_iota(score_shape) % STEPS == 0) & (lane_iota(score_shape) == second)

    def updated(head, side):
        old = load(head, side)
        ones = [fresh[side, :, head_lanes(head)].astype(jnp.float32)[t : t + 1] for t in range(STEPS)]
        new = jnp.where(row == second, ones[1], jnp.where(row == first, ones[0], old.astype(jnp.float32)))
        new = new.astype(jnp.bfloat16)
        keep(head, side, new)
        return jnp.concatenate([new, old], axis=0)

    for head in range(width // HEAD_DIM):
        query = jnp.concatenate([queries[:, head_lanes(head * group_size + i)] for i in range(group_size)], axis=0)
        scores = lax.dot_general(
            query, updated(head, 0), (((1,), (1,)), ((), ())), preferred_element_type=jnp.float32
        )
        scores = jnp.where(stale, scores[:, cache_len:], scores[:, :cache_len]) * HEAD_DIM ** (-0.5)
        weights = jnp.exp(scores - jnp.max(scores, axis=1, keepdims=True))
        weights = weights / jnp.sum(weights, axis=1, keepdims=True)
        both = jnp.concatenate([jnp.where(stale, 0.0, weights), jnp.where(stale, weights, 0.0)], axis=1)
        mixed = jnp.dot(both.astype(jnp.bfloat16), updated(head, 1), preferred_element_type=jnp.float32)
        mixed = mixed.astype(jnp.bfloat16)
        for i in range(group_size):
            store(head * group_size + i, mixed[i * STEPS : (i + 1) * STEPS])


def stay_kernel(counts, hops_in, positions_in, kv, queries, fresh, cache, attended, *scratch):
    hops, positions, plan_sem, buffers, blank, order, load_sems, store_sem = scratch
    load_plan((hops_in, positions_in), (hops, positions), plan_sem)
    slots = kv.shape[0]
    live = counts[0]
    stay = jnp.int32(0)
    for s in range(slots):
        staying = (s < live) & (hops[s] == 0)

        @pl.when(staying)
        def _(s=s, stay=stay):
            order[stay] = s
            pltpu.make_async_copy(kv.at[s], buffers.at[stay], load_sems.at[stay]).start()

        stay = stay + jnp.where(staying, 1, 0)

    blank[...] = jnp.zeros_like(blank)

    def clear(j, carry):
        pltpu.make_async_copy(blank, cache.at[j], store_sem).start()
        attended[j] = jnp.zeros(attended.shape[1:], attended.dtype)
        return carry

    lax.fori_loop(stay, slots, clear, 0)

    def work(j, carry):
        pltpu.make_async_copy(kv.at[0], buffers.at[j], load_sems.at[j]).wait()

        def load(head, side):
            return buffers[j, side, :, head_lanes(head)]

        def keep(head, side, rows):
            buffers[j, side, :, head_lanes(head)] = rows

        def store(head, rows):
            attended[j, :, head_lanes(head)] = rows

        attend(load, keep, positions[order[j]], queries.at[j], fresh.at[j], store)
        pltpu.make_async_copy(buffers.at[j], cache.at[j], store_sem).start()
        return carry

    lax.fori_loop(0, stay, work, 0)

    def drain(j, carry):
        pltpu.make_async_copy(blank, cache.at[0], store_sem).wait()
        return carry

    lax.fori_loop(0, slots, drain, 0)


def arrive_kernel(own, table, queries, fresh, cache_in, attended_in, *refs):
    blocks = refs[: len(ORDER)]
    cache, attended, served, rows, rows_smem, buffers, heads, rows_sem, store_sems = refs[len(ORDER) :]
    del cache_in, attended_in
    groups = table.shape[0]
    cache_len = cache.shape[2]
    here = lax.axis_index("grp")
    headers = {offset: header_of(block) for offset, block in zip(ORDER, blocks)}
    everyone = table[...]
    for offset in ORDER:
        if offset not in NEAR:
            everyone = with_row(everyone, lax.rem(here - offset + groups, groups), headers[offset])
    rows[...] = everyone
    rows_copy = pltpu.make_async_copy(rows, rows_smem, rows_sem)
    rows_copy.start()

    def entry(header, lane):
        shape = header[0:1].shape
        return jnp.sum(jnp.where(lane_iota(shape) == lane, header[0:1], 0))

    places = {}
    place = entry(own[...], STAY)
    for k, offset in enumerate(OFFSETS):
        present = entry(headers[offset], SENT + k) > 0
        places[offset] = (present, place)
        place = place + jnp.where(present, 1, 0)

    def stores(i, slot):
        return (
            pltpu.make_async_copy(buffers.at[i], cache.at[slot], store_sems.at[i, 0]),
            pltpu.make_async_copy(heads.at[i], attended.at[slot], store_sems.at[i, 1]),
        )

    for i, offset in enumerate(ORDER):
        present, slot = places[offset]

        @pl.when(present)
        def _(i=i, slot=slot, offset=offset):
            def load(head, side):
                return blocks[i][block_rows(cache_len, head, side), :]

            def keep(head, side, rows):
                buffers[i, side, :, head_lanes(head)] = rows

            def store(head, rows):
                heads[i, :, head_lanes(head)] = rows

            attend(load, keep, entry(headers[offset], POS), queries.at[slot], fresh.at[slot], store)
            for copy in stores(i, slot):
                copy.start()

    rows_copy.wait()

    def count(g, carry):
        total = rows_smem[g, STAY]
        for k, offset in enumerate(OFFSETS):
            total = total + rows_smem[lax.rem(g - offset + groups, groups), SENT + k]
        served[g] = total
        return carry

    lax.fori_loop(0, groups, count, 0)

    for i, offset in enumerate(ORDER):
        present, slot = places[offset]

        @pl.when(present)
        def _(i=i, slot=slot):
            for copy in stores(i, slot):
                copy.wait()


def per_device(counts, hop_offsets, write_pos, kv_cache, queries, fresh_kv):
    groups = lax.axis_size("grp")
    slots = kv_cache.shape[0]
    stream = kv_cache.shape[1:]
    cache_len, width = stream[1:]
    head_row = queries.shape[1:]
    params = pltpu.CompilerParams(vmem_limit_bytes=VMEM_LIMIT)
    plan = [counts, *(pltpu.with_memory_space_constraint(a, pltpu.HBM) for a in (hop_offsets, write_pos, kv_cache))]
    plan_scratch = [
        pltpu.SMEM(hop_offsets.shape, jnp.int32),
        pltpu.SMEM(write_pos.shape, jnp.int32),
        pltpu.SemaphoreType.DMA,
    ]
    block = jax.ShapeDtypeStruct((width // HEAD_DIM * 2 * cache_len + HEADER, HEAD_DIM), kv_cache.dtype)
    table = jax.ShapeDtypeStruct((groups, LANES), jnp.int32)
    cache = jax.ShapeDtypeStruct(kv_cache.shape, kv_cache.dtype)
    heads = jax.ShapeDtypeStruct(queries.shape, queries.dtype)
    *blocks, own = pl.pallas_call(
        pack_kernel,
        out_shape=[block] * len(ORDER) + [jax.ShapeDtypeStruct((HEADER, LANES), jnp.int32)],
        in_specs=[SMEM_SPEC] + [HBM_SPEC] * 3,
        out_specs=[VMEM_SPEC] * (len(ORDER) + 1),
        scratch_shapes=plan_scratch + [pltpu.SemaphoreType.DMA((len(ORDER),))],
        compiler_params=params,
        name="pack",
    )(*plan)
    arrived = {offset: shifted(block, offset) for offset, block in zip(ORDER, blocks)}

    new_cache, attended = pl.pallas_call(
        stay_kernel,
        out_shape=[cache, heads],
        in_specs=[SMEM_SPEC] + [HBM_SPEC] * 3 + [VMEM_SPEC, VMEM_SPEC],
        out_specs=[ANY_SPEC, VMEM_SPEC],
        scratch_shapes=plan_scratch
        + [
            pltpu.VMEM(kv_cache.shape, kv_cache.dtype),
            pltpu.VMEM(stream, kv_cache.dtype),
            pltpu.SMEM((slots,), jnp.int32),
            pltpu.SemaphoreType.DMA((slots,)),
            pltpu.SemaphoreType.DMA,
        ],
        compiler_params=params,
        cost_estimate=pl.CostEstimate(flops=50_000_000, bytes_accessed=4 * kv_cache.size, transcendentals=0),
        name="stay",
    )(*plan, queries, fresh_kv)

    known = pl.pallas_call(
        relay_kernel,
        out_shape=table,
        in_specs=[VMEM_SPEC] * (1 + len(NEAR)),
        out_specs=VMEM_SPEC,
        compiler_params=params,
        name="relay",
    )(own, *[arrived[offset] for offset in NEAR])
    for distance in relay_shifts(groups):
        known = jnp.maximum(known, shifted(known, distance))

    return pl.pallas_call(
        arrive_kernel,
        out_shape=[cache, heads, jax.ShapeDtypeStruct((groups,), jnp.int32)],
        in_specs=[VMEM_SPEC] * 4 + [ANY_SPEC] * 2 + [VMEM_SPEC] * len(ORDER),
        out_specs=[ANY_SPEC, ANY_SPEC, SMEM_SPEC],
        scratch_shapes=[
            pltpu.VMEM(table.shape, jnp.int32),
            pltpu.SMEM(table.shape, jnp.int32),
            pltpu.VMEM((len(ORDER),) + stream, kv_cache.dtype),
            pltpu.VMEM((len(ORDER),) + head_row, queries.dtype),
            pltpu.SemaphoreType.DMA,
            pltpu.SemaphoreType.DMA((len(ORDER), 2)),
        ],
        input_output_aliases={4: 0, 5: 1},
        compiler_params=params,
        name="arrive",
    )(own, known, queries, fresh_kv, new_cache, attended, *[arrived[offset] for offset in ORDER])


def solution(mesh):
    return jax.shard_map(
        per_device,
        mesh=mesh,
        in_specs=(
            P(("rep", "grp")),
            P(("rep", "grp")),
            P(("rep", "grp")),
            P(("rep", "grp"), None, None, "tp"),
            P(("rep", "grp"), None, "tp"),
            P(("rep", "grp"), None, None, "tp"),
        ),
        out_specs=(P(("rep", "grp"), None, None, "tp"), P(("rep", "grp"), None, "tp"), P("rep")),
        check_vma=False,
    )
```

time: 103 us -> 33.1 us (0.32)
  local copies, waits for them, and re-layouts: 26.3 us -> 0.01 us
  other arithmetic: 21 us -> 0.01 us
  between operations: 15.6 us -> 1.38 us
  Pallas kernels: 0 us -> 13 us
  blocking collectives: 10.6 us -> 0 us
  waiting for transfers between devices: 12.1 us -> 6.64 us
  starting transfers between devices: 14.9 us -> 12.5 us
  matrix products: 2.14 us -> 0 us
    slice x12 -> x0, local copies, waits for them, and re-layouts: 13.6 us -> none  [the longest x4 5.96 us: decode_rows(): current[:, 0].reshape(row_count, cache_len, group_count, HEAD_DIM)]
    pallas_call x0 -> x4, Pallas kernels: none -> 13 us  [the longest x1 8.18 us: per_device(): pl.pallas_call(stay_kernel, out_shape=[cache, heads], in_specs=[SMEM_SPEC...]
    unnamed x1 -> x0, blocking collectives: 10.6 us -> none
    ppermute x8 -> x5, waiting for transfers between devices: 12.1 us -> 6.64 us  [shifted(): lax.ppermute(block, 'grp', [(i, (i + distance) % count) for i in range(co...]
    select_n x5 -> x0, other arithmetic: 4.99 us -> none  [the longest x1 2.85 us: per_device(): jnp.where(filled[:, None, None, None], result_cache, jnp.zeros((), jnp.bf...]
    reduce_sum x3 -> x0, other arithmetic: 4.16 us -> none  [the longest x1 3.3 us: per_device(): served_here = running + jnp.sum(present.astype(jnp.int32))]
    unnamed x35 -> x4, local copies, waits for them, and re-layouts: 3.98 us -> 0.01 us
    gather x2 -> x0, local copies, waits for them, and re-layouts: 2.76 us -> none  [the longest x1 2.12 us: per_device(): placed = jnp.take(pool_rows, source, axis=0)]
  transfers between devices with their start and end apart: 8 -> 5, of which waited for: 4 -> 2; matrix products, arithmetic and copies ran while one was open for 26% -> 0% of each run, Pallas kernels for 0% -> 24%
where the time goes in v1:
time: 33.1 us; the launch traced here: 33.6 us
  Pallas kernels  13 us (39%)
  starting transfers between devices  12.5 us (38%)
  waiting for transfers between devices  6.64 us (20%)
  between operations  1.38 us (4%)
    ppermute x5, starting transfers between devices, shifted(): lax.ppermute(block, 'grp', [(i, (i + distance) % count) for i in range(co...  12.5 us
    pallas_call x1, Pallas kernels, per_device(): pl.pallas_call(stay_kernel, out_shape=[cache, heads], in_specs=[SMEM_SPEC...  8.18 us
    ppermute x5, waiting for transfers between devices, shifted(): lax.ppermute(block, 'grp', [(i, (i + distance) % count) for i in range(co...  6.64 us
    pallas_call x1, Pallas kernels, per_device(): pl.pallas_call(arrive_kernel, out_shape=[cache, heads, jax.ShapeDtypeStru...  2.9 us
    pallas_call x1, Pallas kernels, per_device(): pl.pallas_call(pack_kernel, out_shape=[block] * len(ORDER) + [jax.ShapeDt...  1.92 us
  transfers between devices with their start and end apart: 5, of which 2 were waited for; matrix products, arithmetic and copies ran while one was open for 0% of the time, Pallas kernels for 24%

profile of v1, /device:TPU:0, one launch (start us, length us, event | category | flops | bytes accessed | tf_op | source)
XLA Modules:
  0.0 33.6 jit_solution(7180529953588614606)
XLA Ops:
  0.6 0.0 copy-start.1
  0.6 0.0 copy-start
  1.3 1.9 %pack.1 = (bf16[1040,128]{1,0:T(8,128)(2,1)S(1)}, bf16[1040,128]{1,0:T(8,128)(2,1)S(1)}, bf16[1040,128]{1,0:T(8,128)(2,1)S(1)}, bf16[1040,128]{1,0:T(8,128)(2,1)S(1)}, s32[16,128]{1,0:T(8,128)S(1)}) custom-call(s32[1]{0:T(128)S(6)} %copy.13.counts, s32[8]{0:T(128)} %hops_in.3, s32[8]{0:T(128)} %positions_in.3, bf16[8,2,128,512]{3,2,1,0:T(8,128)(2,1)} %kv.3), custom_call_target="tpu_custom_call" | custom-call | tf_op jit(solution)/shard_map/pack/pallas_call | solution.py:305
  3.3 3.2 %collective-permute-start = (bf16[1040,128]{1,0:T(8,128)(2,1)S(1)}, bf16[1040,128]{1,0:T(8,128)(2,1)S(1)}, u32[]{:S(2)}, u32[]{:S(2)}) collective-permute-start(bf16[1040,128]{1,0:T(8,128)(2,1)S(1)} %get-tuple-element.11), channel_id=1, source_target_pairs={{0,2},{2,4},{4,6},{6,8},{8,10},{10,12},{12,14},{14,0},{1,3},{3,5},... | collective-permute-start | bytes 798728 | tf_op jit(solution)/shard_map/ppermute | solution.py:32
  6.5 3.1 %collective-permute-start.1 = (bf16[1040,128]{1,0:T(8,128)(2,1)S(1)}, bf16[1040,128]{1,0:T(8,128)(2,1)S(1)}, u32[]{:S(2)}, u32[]{:S(2)}) collective-permute-start(bf16[1040,128]{1,0:T(8,128)(2,1)S(1)} %get-tuple-element.12), channel_id=1, source_target_pairs={{0,14},{2,0},{4,2},{6,4},{8,6},{10,8},{12,10},{14,12},{1,15},{3,1}... | collective-permute-start | bytes 798728 | tf_op jit(solution)/shard_map/ppermute | solution.py:32
  9.6 0.0 collective-permute-start.3
  9.6 3.8 %collective-permute-start.4 = (bf16[1040,128]{1,0:T(8,128)(2,1)S(1)}, bf16[1040,128]{1,0:T(8,128)(2,1)S(1)}, u32[]{:S(2)}, u32[]{:S(2)}) collective-permute-start(bf16[1040,128]{1,0:T(8,128)(2,1)S(1)} %get-tuple-element.16), channel_id=1, source_target_pairs={{0,12},{2,14},{4,0},{6,2},{8,4},{10,6},{12,8},{14,10},{1,13},{3,15... | collective-permute-start | bytes 798728 | tf_op jit(solution)/shard_map/ppermute | solution.py:32
  13.4 4.4 %collective-permute-done.refs_0_ = bf16[1040,128]{1,0:T(8,128)(2,1)S(1)} collective-permute-done((bf16[1040,128]{1,0:T(8,128)(2,1)S(1)}, bf16[1040,128]{1,0:T(8,128)(2,1)S(1)}, u32[]{:S(2)}, u32[]{:S(2)}) %collective-permute-start) | collective-permute-done | bytes 266272 | tf_op jit(solution)/shard_map/ppermute | solution.py:32
  17.9 2.2 %collective-permute-done.1.refs_1_ = bf16[1040,128]{1,0:T(8,128)(2,1)S(1)} collective-permute-done((bf16[1040,128]{1,0:T(8,128)(2,1)S(1)}, bf16[1040,128]{1,0:T(8,128)(2,1)S(1)}, u32[]{:S(2)}, u32[]{:S(2)}) %collective-permute-start.1) | collective-permute-done | bytes 266272 | tf_op jit(solution)/shard_map/ppermute | solution.py:32
  20.1 2.3 %collective-permute-start.2 = (s32[8,128]{1,0:T(8,128)S(1)}, s32[8,128]{1,0:T(8,128)S(1)}, u32[]{:S(2)}, u32[]{:S(2)}) collective-permute-start(s32[8,128]{1,0:T(8,128)S(1)} %relay.1), channel_id=1, source_target_pairs={{0,8},{2,10},{4,12},{6,14},{8,0},{10,2},{12,4},{14,6},{1,9},{3,11}... | collective-permute-start | bytes 12296 | tf_op jit(solution)/shard_map/ppermute | solution.py:32
  22.4 0.0 copy-done.1
  22.4 0.0 copy-done
  22.4 8.2 %stay.1 = (bf16[8,2,128,512]{3,2,1,0:T(8,128)(2,1)}, bf16[8,2,4096]{2,1,0:T(2,128)(2,1)}) custom-call(s32[1]{0:T(128)S(6)} %copy.13.counts, s32[8]{0:T(128)} %hops_in.3, s32[8]{0:T(128)} %positions_in.3, bf16[8,2,128,512]{3,2,1,0:T(8,128)(2,1)} %kv.3, bf16[8,2,4096]{2,1,0:T(2,128)(2,1)S(1)} %copy-done, bf16[8,2,2,512]{3,2,1,0:T(2,128)(2,1)S(1)} %copy-done.1), custom_call_target="tpu_custom_call" | custom-call | flops 50000000 | bytes 4194304 | tf_op jit(solution)/shard_map/stay/pallas_call | solution.py:316
  30.6 0.0 collective-permute-done.2
  30.6 0.0 collective-permute-done.3.refs_2_
  30.6 0.0 collective-permute-done.4.refs_3_
  30.7 2.9 %arrive.1 = (bf16[8,2,128,512]{3,2,1,0:T(8,128)(2,1)}, bf16[8,2,4096]{2,1,0:T(2,128)(2,1)}, s32[8]{0:T(128)}) custom-call(s32[16,128]{1,0:T(8,128)S(1)} %get-tuple-element.10.own, s32[8,128]{1,0:T(8,128)S(1)} %max.3.table, bf16[8,2,4096]{2,1,0:T(2,128)(2,1)S(1)} %copy-done, ...), custom_call_target="tpu_custom_call", output_to_operand_aliasing={{0}: (4, {}), {1}: (5, {})} | custom-call | tf_op jit(solution)/shard_map/arrive/pallas_call | solution.py:345
  (2 shorter events, 0.0 us)
Async XLA Ops:
  0.6 21.8 %copy-start.1 = (bf16[8,2,2,512]{3,2,1,0:T(2,128)(2,1)S(1)}, bf16[8,2,2,512]{3,2,1,0:T(2,128)(2,1)}, u32[]{:S(2)}) copy-start(bf16[8,2,2,512]{3,2,1,0:T(2,128)(2,1)} %fresh.3) | copy-start | bytes 98308
  0.6 21.8 %copy-start = (bf16[8,2,4096]{2,1,0:T(2,128)(2,1)S(1)}, bf16[8,2,4096]{2,1,0:T(2,128)(2,1)}, u32[]{:S(2)}) copy-start(bf16[8,2,4096]{2,1,0:T(2,128)(2,1)} %queries.3) | copy-start | bytes 393220
  3.3 14.6 %collective-permute-start = (bf16[1040,128]{1,0:T(8,128)(2,1)S(1)}, bf16[1040,128]{1,0:T(8,128)(2,1)S(1)}, u32[]{:S(2)}, u32[]{:S(2)}) collective-permute-start(bf16[1040,128]{1,0:T(8,128)(2,1)S(1)} %get-tuple-element.11), channel_id=1, source_target_pairs={{0,2},{2,4},{4,6},{6,8},{8,10},{10,12},{12,14},{14,0},{1,3},{3,5},... | collective-permute-start | bytes 798728 | tf_op jit(solution)/shard_map/ppermute | solution.py:32
  6.5 13.6 %collective-permute-start.1 = (bf16[1040,128]{1,0:T(8,128)(2,1)S(1)}, bf16[1040,128]{1,0:T(8,128)(2,1)S(1)}, u32[]{:S(2)}, u32[]{:S(2)}) collective-permute-start(bf16[1040,128]{1,0:T(8,128)(2,1)S(1)} %get-tuple-element.12), channel_id=1, source_target_pairs={{0,14},{2,0},{4,2},{6,4},{8,6},{10,8},{12,10},{14,12},{1,15},{3,1}... | collective-permute-start | bytes 798728 | tf_op jit(solution)/shard_map/ppermute | solution.py:32
  9.6 21.0 %collective-permute-start.3 = (bf16[1040,128]{1,0:T(8,128)(2,1)S(1)}, bf16[1040,128]{1,0:T(8,128)(2,1)S(1)}, u32[]{:S(2)}, u32[]{:S(2)}) collective-permute-start(bf16[1040,128]{1,0:T(8,128)(2,1)S(1)} %get-tuple-element.15), channel_id=1, source_target_pairs={{0,4},{2,6},{4,8},{6,10},{8,12},{10,14},{12,0},{14,2},{1,5},{3,7},... | collective-permute-start | bytes 798728 | tf_op jit(solution)/shard_map/ppermute | solution.py:32
  9.6 21.0 %collective-permute-start.4 = (bf16[1040,128]{1,0:T(8,128)(2,1)S(1)}, bf16[1040,128]{1,0:T(8,128)(2,1)S(1)}, u32[]{:S(2)}, u32[]{:S(2)}) collective-permute-start(bf16[1040,128]{1,0:T(8,128)(2,1)S(1)} %get-tuple-element.16), channel_id=1, source_target_pairs={{0,12},{2,14},{4,0},{6,2},{8,4},{10,6},{12,8},{14,10},{1,13},{3,15... | collective-permute-start | bytes 798728 | tf_op jit(solution)/shard_map/ppermute | solution.py:32
  20.1 10.5 %collective-permute-start.2 = (s32[8,128]{1,0:T(8,128)S(1)}, s32[8,128]{1,0:T(8,128)S(1)}, u32[]{:S(2)}, u32[]{:S(2)}) collective-permute-start(s32[8,128]{1,0:T(8,128)S(1)} %relay.1), channel_id=1, source_target_pairs={{0,8},{2,10},{4,12},{6,14},{8,0},{10,2},{12,4},{14,6},{1,9},{3,11}... | collective-permute-start | bytes 12296 | tf_op jit(solution)/shard_map/ppermute | solution.py:32
